TPU v7x, 256 devices: a whole 4x4x8 slice. The times are simulated.
256 devices in a mesh: dp: 4 (over x_lo, core), cent: 64 (over z, y, x_hi).
Axes of the slice: x: 4 (x_hi: 2, x_lo: 2; x = x_hi * 2 + x_lo), y: 4, z: 8, core: 2. Of those that a mesh axis runs over, the one named last changes fastest.
Arguments:
- embeddings: bfloat16 [8192, 768], P('dp'), may hold values from -40 to 40
- centroids: float32 [65536, 768], P('cent'), may hold values from -0.5 to 0.5
Outputs:
- new_centroids: float32 [65536, 768], P('cent')
- log_total: float32 [8192], P('dp')
All inputs are finite; a program needn't handle non-finite values.
Results may differ from a plain program's by a relative error of at most 0.012.
The roundings to bfloat16 on the way count: a program that leaves them out, or rounds other values in their place, can miss the bound.
Values sent between devices are 32-bit elements; how exact they have to be, the bound alone decides.
A program may use at most 64 MiB of HBM per device.

v0:
```python
import jax
import jax.numpy as jnp
from jax import lax
from jax.sharding import PartitionSpec as P

ITERS = 2


logit_divisor = 0.05
prior = 0.5


def local(embeddings, centroids):
    current = centroids
    log_total = jnp.zeros((embeddings.shape[0],), jnp.float32)
    for step in range(ITERS):
        rounded = current.astype(jnp.bfloat16)
        pairwise_dots = jnp.dot(embeddings, rounded.T, preferred_element_type=jnp.float32)
        semi_length_energy = 0.5 * jnp.sum(current * current, axis=1)
        cluster_logits = (pairwise_dots - semi_length_energy[None, :]) / logit_divisor
        row_max = lax.pmax(jnp.max(cluster_logits, axis=1), "cent")
        row_total = lax.psum(jnp.sum(jnp.exp(cluster_logits - row_max[:, None]), axis=1), "cent")
        weights = (jnp.exp(cluster_logits - row_max[:, None]) / row_total[:, None]).astype(
            jnp.bfloat16
        )
        sums = lax.dot_general(
            weights, embeddings, (((0,), (0,)), ((), ())), preferred_element_type=jnp.float32
        )
        mass = jnp.sum(weights, axis=0, dtype=jnp.float32)
        sums, mass = lax.psum((sums, mass), "dp")
        current = (sums + prior * current) / (mass + prior)[:, None]
        log_total = row_max + jnp.log(row_total)
    return (current, log_total)


def solution(mesh):
    placed = (P("dp", None), P("cent", None))
    return jax.shard_map(
        local, mesh=mesh, in_specs=placed, out_specs=(P("cent", None), P("dp")), check_vma=False
    )
```

profile of v0, /device:TPU:1, one launch (start us, length us, event | category | flops | bytes accessed | tf_op | source)
XLA Modules:
  0.0 952.2 jit_solution(15519896813986065414)
XLA Ops:
  7.2 0.0 copy-start
  7.2 0.0 all-reduce.3.cloned.1.call-start
  7.2 2.3 multiply_reduce_fusion.1
  9.6 0.5 copy-done
  10.0 7.5 fusion
  17.5 162.3 %pmax.14 = f32[2048]{0:T(1024)S(1)} all-reduce(f32[2048]{0:T(1024)S(1)} %get-tuple-element.8), channel_id=1, replica_groups=mesh['dp'=4,'cent'=64] {'cent'}, use_global_device_ids=true, to_apply=%region_2.0 | all-reduce | flops 2048 | bytes 16384 | tf_op jit(solution)/shard_map/pmax | solution.py:21
  179.9 4.5 fusion.2
  184.4 150.7 %psum.42 = f32[2048]{0:T(1024)S(1)} all-reduce(f32[2048]{0:T(1024)S(1)} %fusion.2), channel_id=1, replica_groups=mesh['dp'=4,'cent'=64] {'cent'}, use_global_device_ids=true, to_apply=%region_4.0 | all-reduce | flops 2048 | bytes 16384 | tf_op jit(solution)/shard_map/psum | solution.py:22
  335.1 4.7 convert_reduce_fusion.1
  339.9 5.1 fusion.8
  344.9 0.0 all-reduce.3.cloned.1.call-update
  345.0 0.0 all-reduce.5.cloned.1.call-start
  345.0 61.3 %psum.44 = f32[1024]{0:T(1024)S(1)} all-reduce(f32[1024]{0:T(1024)S(1)} %get-tuple-element.6), channel_id=1, replica_groups=mesh['dp'=4,'cent'=64] {'dp'}, use_global_device_ids=true, to_apply=%region_7.0 | all-reduce | flops 1024 | bytes 8192 | tf_op jit(solution)/shard_map/psum | solution.py:30
  406.3 69.4 %all-reduce.3.cloned.1.call-done = f32[1024,768]{1,0:T(8,128)} async-done(((f32[1024,768]{1,0:T(8,128)}), f32[1024,768]{1,0:T(8,128)}) %all-reduce.3.cloned.1.call-update) | async-done | bytes 3145744 | tf_op jit(solution)/shard_map/psum | solution.py:30
  475.7 3.5 multiply_reduce_fusion
  479.2 0.0 copy-start.1
  479.2 5.7 fusion.1
  484.9 0.0 copy-done.1
  484.9 159.0 %pmax.15 = f32[2048]{0:T(1024)S(1)} all-reduce(f32[2048]{0:T(1024)S(1)} %get-tuple-element.10), channel_id=1, replica_groups=mesh['dp'=4,'cent'=64] {'cent'}, use_global_device_ids=true, to_apply=%region_10.0 | all-reduce | flops 2048 | bytes 16384 | tf_op jit(solution)/shard_map/pmax | solution.py:21
  643.9 4.5 fusion.3
  648.4 151.6 %psum.45 = f32[2048]{0:T(1024)S(1)} all-reduce(f32[2048]{0:T(1024)S(1)} %fusion.3), channel_id=1, replica_groups=mesh['dp'=4,'cent'=64] {'cent'}, use_global_device_ids=true, to_apply=%region_12.0 | all-reduce | flops 2048 | bytes 16384 | tf_op jit(solution)/shard_map/psum | solution.py:22
  800.0 4.7 convert_reduce_fusion
  804.8 5.1 fusion.9
  809.9 0.0 all-reduce.5.cloned.1.call-update
  809.9 59.9 %psum.47 = f32[1024]{0:T(1024)S(1)} all-reduce(f32[1024]{0:T(1024)S(1)} %get-tuple-element.2), channel_id=1, replica_groups=mesh['dp'=4,'cent'=64] {'dp'}, use_global_device_ids=true, to_apply=%region_15.0 | all-reduce | flops 1024 | bytes 8192 | tf_op jit(solution)/shard_map/psum | solution.py:30
  869.8 0.6 log_add_fusion
  870.4 70.0 %all-reduce.5.cloned.1.call-done = f32[1024,768]{1,0:T(8,128)} async-done(((f32[1024,768]{1,0:T(8,128)}), f32[1024,768]{1,0:T(8,128)}) %all-reduce.5.cloned.1.call-update) | async-done | bytes 3145744 | tf_op jit(solution)/shard_map/psum | solution.py:30
  940.4 4.9 add_divide_fusion
  (4 shorter events, 0.0 us)
Async XLA Ops:
  7.2 2.8 copy-start
  7.2 468.5 %all-reduce.3.cloned.1.call-start = ((), (), s32[]{:S(2)}) async-start(), calls=%async_computation | async-start | bytes 6291456 | tf_op jit(solution)/shard_map/psum | solution.py:30
  345.0 595.5 %all-reduce.5.cloned.1.call-start = ((), (), s32[]{:S(2)}) async-start(), calls=%async_computation.1 | async-start | bytes 6291456 | tf_op jit(solution)/shard_map/psum | solution.py:30
  479.2 5.7 copy-start.1
Sparse Core Ops, SparseCore 0:
  345.1 130.5 all-reduce.2
  810.0 130.3 all-reduce.4
where the time goes:
time: 952 us
  blocking collectives  745 us (78%)
  waiting for transfers between devices  139 us (15%)
  other arithmetic  29.8 us (3%)
  matrix products  23.3 us (2%)
  between operations  14.1 us (1%)
    pmax x2, blocking collectives, local(): row_max = lax.pmax(jnp.max(cluster_logits, axis=1), 'cent')  321 us
    psum x2, blocking collectives, local(): lax.psum(jnp.sum(jnp.exp(cluster_logits - row_max[:, None]), axis=1), 'ce...  302 us
    psum x2, waiting for transfers between devices, local(): sums, mass = lax.psum((sums, mass), 'dp')  139 us
    psum x2, blocking collectives, local(): sums, mass = lax.psum((sums, mass), 'dp')  121 us
  transfers between devices with their start and end apart: 2, of which 2 were waited for; matrix products, arithmetic and copies ran while one was open for 0% of the time, Pallas kernels for 0%

commit v1 on v0

v1 whole, which is shorter than its diff:
```python
import jax
import jax.numpy as jnp
from jax import lax
from jax.experimental import pallas as pl
from jax.experimental.pallas import tpu as pltpu
from jax.sharding import PartitionSpec as P

MESH = pl.DeviceIdType.MESH
ITERS = 2
LOG2E = 1.4426950408889634
LN2 = 0.6931471805599453
SCALE = 20.0 * LOG2E
PRIOR = 0.5
D = 768
K = 1024
H = 512
R = 2048
UNIT = 256
PIECE = 32
STEPS = 16
CHUNK = 128
NT = (((1,), (1,)), ((), ()))


def place(x, y, z, core):
    x, y, z = lax.rem(x, 4), lax.rem(y, 4), lax.rem(z, 8)
    return (lax.rem(x, 2) * 2 + core, (z * 4 + y) * 2 + x // 2)


def kernel(
    e_hbm, c_hbm, out_c, out_l,
    e, land, sb, c, cb, nrm, p, ml, z1, z2, mid, tot, s, mass, rs, rsm, wbuf, d0, d1,
    esem, csem, osem, gsend, grecv, s1s, s1r, s2s, s2r, fs, fr, rss, rsr, ms, mr, ags, agr,
):
    dp, ct = lax.axis_index("dp"), lax.axis_index("cent")
    core, xlo = lax.rem(dp, 2), dp // 2
    xhi, y, z = lax.rem(ct, 2), lax.rem(ct // 2, 4), ct // 8
    x = xhi * 2 + xlo
    f1 = lax.rem(y + 2 * z, 4)
    f2 = lax.rem(z + 2 * y, 4)

    twin = place(x, y, z, 1 - core)
    xp, xm = place(x + 1, y, z, core), place(x + 3, y, z, core)
    yp, ym = place(x, y + 1, z, core), place(x, y + 3, z, core)
    zp, zm = place(x, y, z + 1, core), place(x, y, z + 7, core)
    partner = (lax.rem(dp + 2, 4), ct)
    zpeers = [place(x, y, z + k, core) for k in range(1, 8)]
    ypeers = [place(x, y + k, z, core) for k in range(1, 4)]
    ypeers += [place(x + 2, y + k, z, core) for k in range(4)]

    ecopy = pltpu.make_async_copy(e_hbm, e.at[pl.ds(0, R)], esem)
    ecopy.start()
    ccopy = pltpu.make_async_copy(c_hbm, c, csem)
    ccopy.start()

    barrier = pltpu.get_barrier_semaphore()
    peers = [twin, xp, xm] + zpeers + ypeers
    for peer in peers:
        pl.semaphore_signal(barrier, inc=1, device_id=peer, device_id_type=MESH)

    def rows(start, size):
        return pl.ds(pl.multiple_of(start, size), size)

    def remote(src, dst, ssem, rsem, to):
        return pltpu.make_async_remote_copy(
            src_ref=src, dst_ref=dst, send_sem=ssem, recv_sem=rsem, device_id=to, device_id_type=MESH
        )

    def unit_of(t):
        return jnp.where(t < 6, t, 7)

    def piece(u, half, q):
        return rows(u * UNIT + half * 128 + q * PIECE, PIECE)

    ecopy.wait()
    pl.semaphore_wait(barrier, len(peers))

    @pl.loop(0, 7)
    def _(t):
        u = unit_of(t)
        for half, q, to in ((0, f1, xm), (1, f2, xp)):
            src = sb.at[rows(t * 64 + half * 32, 32)]
            src[...] = e[piece(u, half, q), :].astype(jnp.float32)
            remote(
                src, land.at[piece(u, half, q)],
                gsend.at[42 + 2 * t + half], grecv.at[u * 8 + half * 4 + q], to,
            ).start()

    for half, to in ((0, xm), (1, xp)):
        src = sb.at[pl.ds(448 + half * 128, 128)]
        src[...] = e[pl.ds(6 * UNIT + half * 128, 128), :].astype(jnp.float32)
        remote(
            src, land.at[pl.ds(6 * UNIT + half * 128, 128)],
            gsend.at[56 + half], grecv.at[48 + half], to,
        ).start()

    def got(u, half, q):
        remote(
            land.at[piece(u, half, q)], land.at[piece(u, half, q)],
            gsend.at[0], grecv.at[u * 8 + half * 4 + q], twin,
        ).wait_recv()

    def forward(t):
        u = unit_of(t)
        odd = lax.rem(t, 2)
        got(u, 0, f1)
        got(u, 1, f2)
        zone = tuple(jnp.where(odd == 0, a, b) for a, b in zip(zp, zm))
        yone = tuple(jnp.where(odd == 0, a, b) for a, b in zip(yp, ym))
        sends = ((0, f1, yp), (1, f2, zp), (0, f1, ym), (1, f2, zm), (0, f1, zone), (1, f2, yone))
        for j, (half, q, to) in enumerate(sends):
            ref = land.at[piece(u, half, q)]
            remote(ref, ref, gsend.at[t * 6 + j], grecv.at[u * 8 + half * 4 + q], to).start()

    def arrive(u):
        @pl.when(u == 6)
        def _():
            for half in range(2):
                ref = land.at[pl.ds(6 * UNIT + half * 128, 128)]
                remote(ref, ref, gsend.at[0], grecv.at[48 + half], twin).wait_recv()

        @pl.when(u != 6)
        def _():
            for k in range(1, 4):
                got(u, 0, lax.rem(f1 + k, 4))
                got(u, 1, lax.rem(f2 + k, 4))

        e[rows(R + u * UNIT, UNIT), :] = land[rows(u * UNIT, UNIT), :].astype(jnp.bfloat16)

    ccopy.wait()

    def merge(ref, it):
        top = ref[it, 0, 0:8, :]
        for k in range(1, 8):
            top = jnp.maximum(top, ref[it, k, 0:8, :])
        total = jnp.zeros_like(top)
        for k in range(8):
            total += ref[it, k, 8:16, :] * jnp.exp2(ref[it, k, 0:8, :] - top)
        return top, total

    def stats_first(it):
        z1[it, z] = ml[0:16, :]
        for k, to in enumerate(zpeers):
            remote(z1.at[it, z], z1.at[it, z], s1s.at[it * 8 + k], s1r.at[it * 8 + z], to).start()

    def stats_second(it):
        for k in range(1, 8):
            src = lax.rem(z + k, 8)
            remote(z1.at[it, src], z1.at[it, src], s1s.at[0], s1r.at[it * 8 + src], twin).wait_recv()
        top, total = merge(z1, it)
        mid[it, 0:8, :] = top
        mid[it, 8:16, :] = total
        slot = y * 2 + xhi
        z2[it, slot] = mid[it]
        for k, to in enumerate(ypeers):
            remote(mid.at[it], z2.at[it, slot], s2s.at[it * 8 + k], s2r.at[it * 8 + slot], to).start()

    def stats_last(it):
        slot = y * 2 + xhi
        for k in range(1, 8):
            src = lax.rem(slot + k, 8)
            remote(z2.at[it, src], z2.at[it, src], s2s.at[0], s2r.at[it * 8 + src], twin).wait_recv()
        top, total = merge(z2, it)
        tot[it, 0:8, :] = top
        tot[it, 8:16, :] = total
        share(it).start()

    def share(it):
        return remote(tot.at[it, pl.ds(0, 16)], tot.at[it, pl.ds(16, 16)], fs.at[it], fr.at[it], partner)

    def prepare():
        @pl.loop(0, K // CHUNK)
        def _(k):
            at = rows(k * CHUNK, CHUNK)
            block = c[at, :]
            cb[at, :] = block.astype(jnp.bfloat16)
            nrm[at, :] = jnp.broadcast_to(0.5 * jnp.sum(block * block, axis=1, keepdims=True), (CHUNK, 128))

    def dot(u):
        return lax.dot_general(cb[...], e[rows(u * UNIT, UNIT), :], NT, preferred_element_type=jnp.float32)

    def soft(d, u):
        n = nrm[...]
        t = (d - jnp.concatenate([n, n], axis=1)) * SCALE
        m = jnp.max(t, axis=0, keepdims=True)
        w = jnp.exp2(t - m)
        p[u] = w
        at = (u // 8) * 16 + lax.rem(u, 8)
        ml[pl.ds(at, 1), :] = m
        ml[pl.ds(at + 8, 1), :] = jnp.sum(w, axis=0, keepdims=True)

    def scores(g):
        d0[...] = dot(2 * g)
        d1[...] = dot(2 * g + 1)
        soft(d0[...], 2 * g)
        soft(d1[...], 2 * g + 1)

    def weigh(g, it):
        side = g // 4

        @pl.when(lax.rem(g, 4) == 0)
        def _():
            s[side] = jnp.zeros((K, D), jnp.float32)
            mass[side] = jnp.zeros((K, 128), jnp.float32)

        total = mass[side]
        for j in range(2):
            at = side * 16 + lax.rem(2 * g, 8) + j
            part = jnp.exp2(ml[pl.ds(at, 1), :] - tot[it, pl.ds(at, 1), :]) / tot[it, pl.ds(at + 8, 1), :]
            w = (p[2 * g + j] * part).astype(jnp.bfloat16)
            wide = w.astype(jnp.float32)
            total += wide[:, :128] + wide[:, 128:]
            wbuf[:, j * UNIT : (j + 1) * UNIT] = w
        mass[side] = total
        s[side] += jnp.dot(wbuf[...], e[rows(g * 512, 512), :], preferred_element_type=jnp.float32)

    def update(it):
        mine, theirs = core * H, (1 - core) * H
        n = H // CHUNK

        @pl.loop(0, n)
        def _(k):
            at = rows(theirs + k * CHUNK, CHUNK)
            to = rows(k * CHUNK, CHUNK)
            s[0, at, :] += s[1, at, :]
            mass[0, at, :] += mass[1, at, :]
            remote(s.at[0, at], rs.at[to], rss.at[it * n + k], rsr.at[it * n + k], twin).start()
            remote(mass.at[0, at], rsm.at[to], ms.at[it * n + k], mr.at[it * n + k], twin).start()

        @pl.loop(0, n)
        def _(k):
            at = rows(mine + k * CHUNK, CHUNK)
            to = rows(k * CHUNK, CHUNK)
            remote(s.at[0, at], rs.at[to], rss.at[it * n + k], rsr.at[it * n + k], twin).wait_recv()
            remote(mass.at[0, at], rsm.at[to], ms.at[it * n + k], mr.at[it * n + k], twin).wait_recv()
            full = (mass[0, at, :] + mass[1, at, :]) + rsm[to, :]
            scale = 1.0 / (jnp.sum(full, axis=1, keepdims=True) + PRIOR)
            c[at, :] = ((s[0, at, :] + s[1, at, :]) + rs[to, :] + PRIOR * c[at, :]) * scale

            @pl.when(it == 0)
            def _():
                remote(c.at[at], c.at[at], ags.at[k], agr.at[k], twin).start()

            @pl.when(it == 1)
            def _():
                remote(c.at[at], out_c.at[at], ags.at[n + k], agr.at[n + k], twin).start()
                pltpu.make_async_copy(c.at[at], out_c.at[at], osem.at[k]).start()

        @pl.loop(0, n)
        def _(k):
            at = rows(theirs + k * CHUNK, CHUNK)
            to = rows(k * CHUNK, CHUNK)
            remote(s.at[0, at], rs.at[to], rss.at[it * n + k], rsr.at[it * n + k], twin).wait_send()
            remote(mass.at[0, at], rsm.at[to], ms.at[it * n + k], mr.at[it * n + k], twin).wait_send()

            @pl.when(it == 0)
            def _():
                remote(c.at[at], c.at[at], ags.at[k], agr.at[k], twin).wait()

            @pl.when(it == 1)
            def _():
                remote(c.at[at], out_c.at[at], ags.at[n + k], agr.at[n + k], twin).wait()
                pltpu.make_async_copy(c.at[at], out_c.at[at], osem.at[k]).wait()

    @pl.loop(0, ITERS * STEPS)
    def _(step):
        it, r = step // STEPS, lax.rem(step, STEPS)
        first = it == 0
        late = jnp.logical_and(first, r >= 12)
        split = jnp.where(first, 6, 8)
        is_scores = jnp.where(late, lax.rem(r, 2) == 0, r < split)
        g = jnp.where(late, 6 + (r - 12) // 2, jnp.where(r < split, r, r - split))

        def at(cond):
            return pl.when(cond)

        @at(r == 0)
        def _():
            prepare()

        @at(jnp.logical_and(first, jnp.logical_or(r == 2, r == 3)))
        def _():
            forward(r - 2)

        @at(r == 4)
        def _():
            stats_first(it)

        @at(jnp.logical_and(first, jnp.logical_or(r == 4, r == 5)))
        def _():
            forward(2 * r - 6)

        @at(r == jnp.where(first, 5, 6))
        def _():
            stats_second(it)

        @at(jnp.logical_and(first, jnp.logical_or(r == 4, r == 5)))
        def _():
            forward(2 * r - 5)

        @at(jnp.logical_and(first, r == 5))
        def _():
            forward(6)

        @at(jnp.logical_and(jnp.logical_and(first, is_scores), g >= 4))
        def _():
            arrive(2 * g - 8)
            arrive(2 * g - 7)

        @at(r == jnp.where(first, 6, 8))
        def _():
            stats_last(it)

        @at(r == jnp.where(first, 10, 12))
        def _():
            share(it).wait_recv()

        @at(is_scores)
        def _():
            scores(g)

        @at(jnp.logical_not(is_scores))
        def _():
            weigh(g, it)

        @at(r == STEPS - 1)
        def _():
            update(it)

    @pl.loop(0, 56)
    def _(k):
        ref = land.at[pl.ds(0, PIECE)]
        remote(ref, ref, gsend.at[k], grecv.at[0], twin).wait_send()

    for half in range(2):
        ref = land.at[pl.ds(0, 128)]
        remote(ref, ref, gsend.at[56 + half], grecv.at[0], twin).wait_send()

    for it in range(ITERS):
        for k in range(7):
            ref = mid.at[0]
            remote(ref, ref, s1s.at[it * 8 + k], s1r.at[0], twin).wait_send()
            remote(ref, ref, s2s.at[it * 8 + k], s2r.at[0], twin).wait_send()
        share(it).wait_send()

    value = (tot[1, 0:8, :] + jnp.log2(tot[1, 8:16, :])) * LN2
    for u in range(8):
        out_l[2 * u : 2 * u + 1, :] = value[u : u + 1, :128]
        out_l[2 * u + 1 : 2 * u + 2, :] = value[u : u + 1, 128:]


def local(embeddings, centroids):
    f32, bf16, dma = jnp.float32, jnp.bfloat16, pltpu.SemaphoreType.DMA
    vmem = pltpu.VMEM
    new, logs = pl.pallas_call(
        kernel,
        out_shape=(jax.ShapeDtypeStruct((K, D), f32), jax.ShapeDtypeStruct((16, 128), f32)),
        in_specs=[pl.BlockSpec(memory_space=pl.ANY)] * 2,
        out_specs=(pl.BlockSpec(memory_space=pl.ANY), pl.BlockSpec(memory_space=pltpu.VMEM)),
        scratch_shapes=[
            vmem((2 * R, D), bf16),
            vmem((R, D), f32),
            vmem((704, D), f32),
            vmem((K, D), f32),
            vmem((K, D), bf16),
            vmem((K, 128), f32),
            vmem((16, K, UNIT), f32),
            vmem((32, UNIT), f32),
            vmem((2, 8, 16, UNIT), f32),
            vmem((2, 8, 16, UNIT), f32),
            vmem((2, 16, UNIT), f32),
            vmem((2, 32, UNIT), f32),
            vmem((2, K, D), f32),
            vmem((2, K, 128), f32),
            vmem((H, D), f32),
            vmem((H, 128), f32),
            vmem((K, 2 * UNIT), bf16),
            vmem((K, UNIT), f32),
            vmem((K, UNIT), f32),
            dma, dma, dma((4,)),
            dma((64,)), dma((64,)),
            dma((16,)), dma((16,)), dma((16,)), dma((16,)),
            dma((2,)), dma((2,)),
            dma((8,)), dma((8,)), dma((8,)), dma((8,)), dma((8,)), dma((8,)),
        ],
        compiler_params=pltpu.CompilerParams(
            collective_id=0, has_side_effects=True, vmem_limit_bytes=60 << 20
        ),
    )(embeddings, centroids)
    return new, logs.reshape(R)


def solution(mesh):
    placed = (P("dp", None), P("cent", None))
    return jax.shard_map(
        local, mesh=mesh, in_specs=placed, out_specs=(P("cent", None), P("dp")), check_vma=False
    )
```

time: 952 us -> 105 us (0.11)
  blocking collectives: 745 us -> 0 us
  waiting for transfers between devices: 139 us -> 0 us
  Pallas kernels: 0 us -> 100 us
  other arithmetic: 29.8 us -> 0 us
  matrix products: 23.3 us -> 0 us
  between operations: 14.1 us -> 0.65 us
    psum x4 -> x0, blocking collectives: 424 us -> none  [the longest x2 302 us: local(): lax.psum(jnp.sum(jnp.exp(cluster_logits - row_max[:, None]), axis=1), 'ce...]
    pmax x2 -> x0, blocking collectives: 321 us -> none  [local(): row_max = lax.pmax(jnp.max(cluster_logits, axis=1), 'cent')]
    psum x2 -> x0, waiting for transfers between devices: 139 us -> none  [local(): sums, mass = lax.psum((sums, mass), 'dp')]
    pallas_call x0 -> x1, Pallas kernels: none -> 100 us  [local(): pl.pallas_call(kernel, out_shape=(jax.ShapeDtypeStruct((K, D), f32), jax....]
    reduce_sum x6 -> x0, other arithmetic: 24.3 us -> none  [the longest x2 9.46 us: local(): mass = jnp.sum(weights, axis=0, dtype=jnp.float32)]
    dot_general x4 -> x0, matrix products: 23.3 us -> none  [the longest x2 13.2 us: local(): jnp.dot(embeddings, rounded.T, preferred_element_type=jnp.float32)]
  transfers between devices with their start and end apart: 2 -> 0, of which waited for: 2 -> 0; matrix products, arithmetic and copies ran while one was open for 0% -> 0% of each run, Pallas kernels for 0% -> 0%
where the time goes in v1:
time: 105 us
  Pallas kernels  100 us (95%)
  local copies, waits for them, and re-layouts  4.36 us (4%)
    pallas_call x1, Pallas kernels, local(): pl.pallas_call(kernel, out_shape=(jax.ShapeDtypeStruct((K, D), f32), jax....  100 us
    unnamed x4, local copies, waits for them, and re-layouts  4.36 us

profile of v1, /device:TPU:1, one launch (start us, length us, event | category | flops | bytes accessed | tf_op | source)
XLA Modules:
  0.0 105.3 jit_solution(1660256737761658343)
XLA Ops:
  0.6 100.3 %shard_map.41 = (f32[1024,768]{1,0:T(8,128)}, f32[16,128]{1,0:T(8,128)}) custom-call(bf16[2048,768]{1,0:T(8,128)(2,1)} %e_hbm.1, f32[1024,768]{1,0:T(8,128)} %c_hbm.1), custom_call_target="tpu_custom_call" | custom-call | tf_op jit(solution)/shard_map/pallas_call | solution.py:355
  100.9 0.0 copy-start
  100.9 3.8 %copy.6 = f32[1024,768]{1,0:T(8,128)} copy(f32[1024,768]{1,0:T(8,128)} %get-tuple-element.8) | data formatting | bytes 6291456
  104.7 0.0 copy-done
  104.7 0.6 copy.7
Async XLA Ops:
  100.9 3.8 %copy-start = (f32[16,128]{1,0:T(8,128)S(1)}, f32[16,128]{1,0:T(8,128)}, u32[]{:S(2)}) copy-start(f32[16,128]{1,0:T(8,128)} %get-tuple-element.5) | copy-start | bytes 24580

commit v2 on v0

v2 whole, which is shorter than its diff:
```python
import jax
import jax.numpy as jnp
from jax import lax
from jax.experimental import pallas as pl
from jax.experimental.pallas import tpu as pltpu
from jax.sharding import PartitionSpec as P

MESH = pl.DeviceIdType.MESH
ITERS = 2
LOG2E = 1.4426950408889634
LN2 = 0.6931471805599453
SCALE = 20.0 * LOG2E
PRIOR = 0.5
D = 768
K = 1024
H = 512
R = 2048
UNIT = 256
PIECE = 32
CHUNK = 128
BLOCK = 256
NT = (((1,), (1,)), ((), ()))


def place(x, y, z, core):
    x, y, z = lax.rem(x, 4), lax.rem(y, 4), lax.rem(z, 8)
    return (lax.rem(x, 2) * 2 + core, (z * 4 + y) * 2 + x // 2)


def kernel(
    e_hbm, c_hbm, out_c, out_t,
    e, land, sb, c, cb, nrm, p, ml, z1, z2, tot, s, mass, rs, rsm, wbuf, d0, d1,
    esem, csem, osem, gsend, grecv, s1s, s1r, s2s, s2r, fs, fr, rss, rsr, ms, mr, ags, agr, relay,
):
    dp, ct = lax.axis_index("dp"), lax.axis_index("cent")
    core, xlo = lax.rem(dp, 2), dp // 2
    xhi, y, z = lax.rem(ct, 2), lax.rem(ct // 2, 4), ct // 8
    x = xhi * 2 + xlo
    f1 = lax.rem(y + 2 * z, 4)
    f2 = lax.rem(z + 2 * y, 4)

    twin = place(x, y, z, 1 - core)
    xp, xm = place(x + 1, y, z, core), place(x + 3, y, z, core)
    yp, ym = place(x, y + 1, z, core), place(x, y + 3, z, core)
    zp, zm = place(x, y, z + 1, core), place(x, y, z + 7, core)
    partner = (lax.rem(dp + 2, 4), ct)
    zpeers = [place(x, y, z + k, core) for k in range(1, 8)]
    ypeers = [place(x, y + k, z, core) for k in range(1, 4)]
    ypeers += [place(x + 2, y + k, z, core) for k in range(4)]

    ecopy = pltpu.make_async_copy(e_hbm, e.at[pl.ds(0, R)], esem)
    ecopy.start()
    ccopy = pltpu.make_async_copy(c_hbm, c, csem)
    ccopy.start()

    barrier = pltpu.get_barrier_semaphore()
    near = [xp, xm, yp, ym, zp, zm]
    for peer in near + [twin]:
        pl.semaphore_signal(barrier, inc=1, device_id=peer, device_id_type=MESH)

    def rows(start, size):
        return pl.ds(pl.multiple_of(start, size), size)

    def remote(src, dst, ssem, rsem, to):
        return pltpu.make_async_remote_copy(
            src_ref=src, dst_ref=dst, send_sem=ssem, recv_sem=rsem, device_id=to, device_id_type=MESH
        )

    def unit_of(t):
        return jnp.where(t < 6, t, 7)

    def piece(u, half, q):
        return rows(u * UNIT + half * 128 + q * PIECE, PIECE)

    ecopy.wait()
    pl.semaphore_wait(barrier, 7)

    def tell(r):
        for peer in near:
            pl.semaphore_signal(relay.at[r], inc=1, device_id=peer, device_id_type=MESH)

    def told(r):
        pl.semaphore_wait(relay.at[r], 6)

    def spread(t):
        u = unit_of(t)
        for half, q, to in ((0, f1, xm), (1, f2, xp)):
            src = sb.at[rows(t * 64 + half * 32, 32)]
            src[...] = e[piece(u, half, q), :].astype(jnp.float32)
            remote(
                src, land.at[piece(u, half, q)],
                gsend.at[42 + 2 * t + half], grecv.at[u * 8 + half * 4 + q], to,
            ).start()

        @pl.when(t == 6)
        def _():
            for half, q, to in ((0, f1 + 2, xm), (1, f2 + 2, xp)):
                q = lax.rem(q, 4)
                src = sb.at[rows(704 + half * 32, 32)]
                src[...] = e[piece(7, half, q), :].astype(jnp.float32)
                remote(
                    src, land.at[piece(7, half, q)], gsend.at[40 + half], grecv.at[56 + half * 4 + q], to
                ).start()

    def spread_whole():
        for half, to in ((0, xm), (1, xp)):
            src = sb.at[pl.ds(448 + half * 128, 128)]
            src[...] = e[pl.ds(6 * UNIT + half * 128, 128), :].astype(jnp.float32)
            remote(
                src, land.at[pl.ds(6 * UNIT + half * 128, 128)],
                gsend.at[56 + half], grecv.at[48 + half], to,
            ).start()

    spread(0)
    tell(0)

    @pl.loop(1, 7)
    def _(t):
        spread(t)

    spread_whole()

    def got(u, half, q):
        remote(
            land.at[piece(u, half, q)], land.at[piece(u, half, q)],
            gsend.at[0], grecv.at[u * 8 + half * 4 + q], twin,
        ).wait_recv()

    def forward(t):
        u = unit_of(t)
        odd = lax.rem(t, 2)
        got(u, 0, f1)
        got(u, 1, f2)
        zone = tuple(jnp.where(odd == 0, a, b) for a, b in zip(zp, zm))
        yone = tuple(jnp.where(odd == 0, a, b) for a, b in zip(yp, ym))
        sends = ((0, f1, yp), (1, f2, zp), (0, f1, ym), (1, f2, zm), (0, f1, zone), (1, f2, yone))

        def send(j):
            half, q, to = sends[j]
            ref = land.at[piece(u, half, q)]
            remote(ref, ref, gsend.at[t * 6 + j], grecv.at[u * 8 + half * 4 + q], to).start()

        for j in range(4):
            send(j)

        @pl.when(t < 6)
        def _():
            send(4)
            send(5)


    def arrive(u):
        @pl.when(u == 6)
        def _():
            for half in range(2):
                ref = land.at[pl.ds(6 * UNIT + half * 128, 128)]
                remote(ref, ref, gsend.at[0], grecv.at[48 + half], twin).wait_recv()

        @pl.when(u != 6)
        def _():
            for k in range(1, 4):
                got(u, 0, lax.rem(f1 + k, 4))
                got(u, 1, lax.rem(f2 + k, 4))

        e[rows(R + u * UNIT, UNIT), :] = land[rows(u * UNIT, UNIT), :].astype(jnp.bfloat16)

    ccopy.wait()

    def prepare(at):
        block = c[at, :]
        cb[at, :] = block.astype(jnp.bfloat16)
        nrm[at, :] = jnp.broadcast_to(0.5 * jnp.sum(block * block, axis=1, keepdims=True), (CHUNK, 128))

    def merge(ref, it, h):
        top = ref[it, h, 0, 0:4, :]
        for k in range(1, 8):
            top = jnp.maximum(top, ref[it, h, k, 0:4, :])
        total = jnp.zeros_like(top)
        for k in range(8):
            total += ref[it, h, k, 4:8, :] * jnp.exp2(ref[it, h, k, 0:4, :] - top)
        return top, total

    def send_all(ref, it, h, slot, ssem, rsem, peers):
        for k, to in enumerate(peers):
            at = (it * 2 + h) * 8
            remote(ref.at[it, h, slot], ref.at[it, h, slot], ssem.at[at + k], rsem.at[at + slot], to).start()

    def receive_all(ref, it, h, slot, ssem, rsem):
        for k in range(1, 8):
            src = lax.rem(slot + k, 8)
            at = (it * 2 + h) * 8 + src
            remote(ref.at[it, h, src], ref.at[it, h, src], ssem.at[0], rsem.at[at], twin).wait_recv()

    def stats_first(it, h):
        z1[it, h, z] = ml[h * 8 : h * 8 + 8, :]
        send_all(z1, it, h, z, s1s, s1r, zpeers)

    yslot = y * 2 + xhi

    def stats_second(it, h):
        receive_all(z1, it, h, z, s1s, s1r)
        top, total = merge(z1, it, h)
        z2[it, h, yslot, 0:4, :] = top
        z2[it, h, yslot, 4:8, :] = total
        send_all(z2, it, h, yslot, s2s, s2r, ypeers)

    def share(it, h):
        src, dst = tot.at[it, pl.ds(h * 8, 8)], tot.at[it, pl.ds(16 + h * 8, 8)]
        return remote(src, dst, fs.at[it * 2 + h], fr.at[it * 2 + h], partner)

    def stats_last(it, h):
        receive_all(z2, it, h, yslot, s2s, s2r)
        top, total = merge(z2, it, h)
        tot[it, h * 8 : h * 8 + 4, :] = top
        tot[it, h * 8 + 4 : h * 8 + 8, :] = total
        share(it, h).start()

    def dot(g):
        return lax.dot_general(cb[...], e[rows(g * 512, 512), :], NT, preferred_element_type=jnp.float32)

    def stat_row(u):
        return (u // 4) * 8 + lax.rem(u, 4)

    def soft(d, g):
        n = nrm[...]
        n = jnp.concatenate([n, n], axis=1)
        for j in range(2):
            u = 2 * g + j
            t = (d[:, j * UNIT : (j + 1) * UNIT] - n) * SCALE
            m = jnp.max(t, axis=0, keepdims=True)
            w = jnp.exp2(t - m)
            p[u] = w
            ml[pl.ds(stat_row(u), 1), :] = m
            ml[pl.ds(stat_row(u) + 4, 1), :] = jnp.sum(w, axis=0, keepdims=True)

    def scores(g):
        d0[...] = dot(g)
        soft(d0, g)

    def weigh(it, u0, n, at):
        total = jnp.zeros((BLOCK, 128), jnp.float32)
        for j in range(n):
            row = stat_row(u0 + j)
            part = jnp.exp2(ml[pl.ds(row, 1), :] - tot[it, pl.ds(row, 1), :]) / tot[it, pl.ds(row + 4, 1), :]
            w = (p[u0 + j, at, :] * part).astype(jnp.bfloat16)
            wide = w.astype(jnp.float32)
            total += wide[:, :128] + wide[:, 128:]
            wbuf[:, j * UNIT : (j + 1) * UNIT] = w
        block = e[rows(u0 * UNIT, n * UNIT), :]
        return jnp.dot(wbuf[:, : n * UNIT], block, preferred_element_type=jnp.float32), total

    def weigh_half(it, side, h, at):
        add, total = weigh(it, 8 * side + 4 * h, 4, at)
        s[side, at, :] = add if h == 0 else s[side, at, :] + add
        mass[side, at, :] = total if h == 0 else mass[side, at, :] + total

    def weigh_own(it, h):
        @pl.loop(0, K // BLOCK)
        def _(k):
            weigh_half(it, 0, h, rows(k * BLOCK, BLOCK))

    mine, theirs = core * H, (1 - core) * H
    n = H // BLOCK

    def update(it):
        def finish_sums(at):
            for h in range(2):
                weigh_half(it, 1, h, at)
            return s[0, at, :] + s[1, at, :], mass[0, at, :] + mass[1, at, :]

        def give(k):
            at, to = rows(theirs + k * BLOCK, BLOCK), rows(k * BLOCK, BLOCK)
            i = it * n + k
            return (
                remote(s.at[0, at], rs.at[to], rss.at[i], rsr.at[i], twin),
                remote(mass.at[0, at], rsm.at[to], ms.at[i], mr.at[i], twin),
            )

        def spread_new(start, i):
            at = rows(start + i * CHUNK, CHUNK)
            dst = c if it == 0 else out_c
            return remote(c.at[at], dst.at[at], ags.at[it * 4 + i], agr.at[it * 4 + i], twin)

        @pl.loop(0, n)
        def _(k):
            at = rows(theirs + k * BLOCK, BLOCK)
            sums, total = finish_sums(at)
            s[0, at, :] = sums
            mass[0, at, :] = total
            for copy in give(k):
                copy.start()

        @pl.loop(0, n)
        def _(k):
            at, to = rows(mine + k * BLOCK, BLOCK), rows(k * BLOCK, BLOCK)
            sums, total = finish_sums(at)
            for copy in give(k):
                copy.wait_recv()
            total = total + rsm[to, :]
            scale = 1.0 / (jnp.sum(total, axis=1, keepdims=True) + PRIOR)
            for j in range(BLOCK // CHUNK):
                sub = rows(mine + k * BLOCK + j * CHUNK, CHUNK)
                cut = slice(j * CHUNK, (j + 1) * CHUNK)
                add = rs[rows(k * BLOCK + j * CHUNK, CHUNK), :]
                c[sub, :] = (sums[cut, :] + add + PRIOR * c[sub, :]) * scale[cut, :]
                spread_new(mine, 2 * k + j).start()
                if it == 0:
                    prepare(sub)
            if it == 1:
                pltpu.make_async_copy(c.at[at], out_c.at[at], osem.at[k]).start()

        @pl.loop(0, n)
        def _(k):
            for copy in give(k):
                copy.wait_send()
            for j in range(BLOCK // CHUNK):
                spread_new(theirs, 2 * k + j).wait()
                if it == 0:
                    prepare(rows(theirs + k * BLOCK + j * CHUNK, CHUNK))
            if it == 1:
                at = rows(mine + k * BLOCK, BLOCK)
                pltpu.make_async_copy(c.at[at], out_c.at[at], osem.at[k]).wait()

    def pipelined(pairs, hook):
        d0[...] = dot(0)

        @pl.loop(0, pairs)
        def _(k):
            d1[...] = dot(2 * k + 1)
            soft(d0, 2 * k)

            @pl.when(k < pairs - 1)
            def _():
                d0[...] = dot(2 * k + 2)
                soft(d1, 2 * k + 1)

            @pl.when(k == pairs - 1)
            def _():
                soft(d1, 2 * pairs - 1)

            hook(k)

    @pl.loop(0, K // CHUNK)
    def _(k):
        prepare(rows(k * CHUNK, CHUNK))

    def meanwhile(k):
        @pl.when(k == 0)
        def _():
            told(0)
            tell(1)

        @pl.when(k == 1)
        def _():
            told(1)
            tell(2)

        forward(k)

    pipelined(2, meanwhile)
    forward(2)
    told(2)
    for h in range(2):
        stats_first(0, h)
    for t in (3, 4):
        forward(t)

    @pl.loop(4, 8)
    def _(g):
        arrive(2 * g - 8)
        arrive(2 * g - 7)
        scores(g)

        @pl.when(g == 4)
        def _():
            for h in range(2):
                stats_second(0, h)

            @pl.loop(5, 7)
            def _(t):
                forward(t)

            for h in range(2):
                stats_last(0, h)
                weigh_own(0, h)

    for h in range(2):
        share(0, h).wait_recv()
    update(0)

    def between(k):
        for h in range(2):

            @pl.when(k == h)
            def _():
                stats_first(1, h)

        @pl.when(k == 2)
        def _():
            stats_second(1, 0)

    pipelined(4, between)
    stats_second(1, 1)
    for h in range(2):
        stats_last(1, h)
        weigh_own(1, h)
    for h in range(2):
        share(1, h).wait_recv()
    update(1)

    @pl.loop(0, 56)
    def _(k):
        ref = land.at[pl.ds(0, PIECE)]
        remote(ref, ref, gsend.at[k], grecv.at[0], twin).wait_send()

    for half in range(2):
        ref = land.at[pl.ds(0, 128)]
        remote(ref, ref, gsend.at[56 + half], grecv.at[0], twin).wait_send()

    for it in range(ITERS):
        for h in range(2):
            ref = z1.at[0, 0, 0]
            for k in range(7):
                remote(ref, ref, s1s.at[(it * 2 + h) * 8 + k], s1r.at[0], twin).wait_send()
                remote(ref, ref, s2s.at[(it * 2 + h) * 8 + k], s2r.at[0], twin).wait_send()
            share(it, h).wait_send()

    out_t[...] = tot[1, 0:16, :]


def finish(c, tot, out_c, out_l, sems):
    copies = []
    for k in range(8):
        at = pl.ds(k * 128, 128)
        copies.append(pltpu.make_async_copy(c.at[at], out_c.at[at], sems.at[k]))
        copies[k].start()
    for h in range(2):
        value = (tot[h * 8 : h * 8 + 4, :] + jnp.log2(tot[h * 8 + 4 : h * 8 + 8, :])) * LN2
        for j in range(4):
            at = 8 * h + 2 * j
            out_l[at : at + 1, :] = value[j : j + 1, :128]
            out_l[at + 1 : at + 2, :] = value[j : j + 1, 128:]
    for copy in copies:
        copy.wait()


def local(embeddings, centroids):
    f32, bf16, dma = jnp.float32, jnp.bfloat16, pltpu.SemaphoreType.DMA
    vmem = pltpu.VMEM
    new, stats = pl.pallas_call(
        kernel,
        out_shape=(jax.ShapeDtypeStruct((K, D), f32), jax.ShapeDtypeStruct((16, UNIT), f32)),
        in_specs=[pl.BlockSpec(memory_space=pl.ANY)] * 2,
        out_specs=(pl.BlockSpec(memory_space=pl.ANY), pl.BlockSpec(memory_space=pltpu.VMEM)),
        scratch_shapes=[
            vmem((2 * R, D), bf16),
            vmem((R, D), f32),
            vmem((768, D), f32),
            vmem((K, D), f32),
            vmem((K, D), bf16),
            vmem((K, 128), f32),
            vmem((16, K, UNIT), f32),
            vmem((32, UNIT), f32),
            vmem((2, 2, 8, 8, UNIT), f32),
            vmem((2, 2, 8, 8, UNIT), f32),
            vmem((2, 32, UNIT), f32),
            vmem((2, K, D), f32),
            vmem((2, K, 128), f32),
            vmem((H, D), f32),
            vmem((H, 128), f32),
            vmem((BLOCK, 4 * UNIT), bf16),
            vmem((K, 2 * UNIT), f32),
            vmem((K, 2 * UNIT), f32),
            dma, dma, dma((4,)),
            dma((64,)), dma((64,)),
            dma((32,)), dma((32,)), dma((32,)), dma((32,)),
            dma((4,)), dma((4,)),
            dma((4,)), dma((4,)), dma((4,)), dma((4,)), dma((8,)), dma((8,)),
            pltpu.SemaphoreType.REGULAR((3,)),
        ],
        compiler_params=pltpu.CompilerParams(
            collective_id=0, has_side_effects=True, vmem_limit_bytes=54 << 20
        ),
    )(embeddings, centroids)
    new, logs = pl.pallas_call(
        finish,
        out_shape=(jax.ShapeDtypeStruct((K, D), f32), jax.ShapeDtypeStruct((16, 128), f32)),
        in_specs=[pl.BlockSpec(memory_space=pl.ANY), pl.BlockSpec(memory_space=vmem)],
        out_specs=(pl.BlockSpec(memory_space=pl.ANY), pl.BlockSpec(memory_space=vmem)),
        scratch_shapes=[dma((8,))],
        compiler_params=pltpu.CompilerParams(vmem_limit_bytes=60 << 20),
    )(new, stats)
    return new, logs.reshape(R)


def solution(mesh):
    placed = (P("dp", None), P("cent", None))
    return jax.shard_map(
        local, mesh=mesh, in_specs=placed, out_specs=(P("cent", None), P("dp")), check_vma=False
    )
```

time: 952 us -> 183 us (0.19)
  blocking collectives: 745 us -> 0 us
  Pallas kernels: 0 us -> 182 us
  waiting for transfers between devices: 139 us -> 0 us
  other arithmetic: 29.8 us -> 0 us
  matrix products: 23.3 us -> 0 us
  between operations: 14.1 us -> 0.8 us
    psum x4 -> x0, blocking collectives: 424 us -> none  [the longest x2 302 us: local(): lax.psum(jnp.sum(jnp.exp(cluster_logits - row_max[:, None]), axis=1), 'ce...]
    pmax x2 -> x0, blocking collectives: 321 us -> none  [local(): row_max = lax.pmax(jnp.max(cluster_logits, axis=1), 'cent')]
    pallas_call x0 -> x2, Pallas kernels: none -> 182 us  [the longest x1 97.8 us: local(): pl.pallas_call(finish, out_shape=(jax.ShapeDtypeStruct((K, D), f32), jax....]
    psum x2 -> x0, waiting for transfers between devices: 139 us -> none  [local(): sums, mass = lax.psum((sums, mass), 'dp')]
    reduce_sum x6 -> x0, other arithmetic: 24.3 us -> none  [the longest x2 9.46 us: local(): mass = jnp.sum(weights, axis=0, dtype=jnp.float32)]
    dot_general x4 -> x0, matrix products: 23.3 us -> none  [the longest x2 13.2 us: local(): jnp.dot(embeddings, rounded.T, preferred_element_type=jnp.float32)]
  transfers between devices with their start and end apart: 2 -> 0, of which waited for: 2 -> 0; matrix products, arithmetic and copies ran while one was open for 0% -> 0% of each run, Pallas kernels for 0% -> 0%
where the time goes in v2:
time: 183 us
  Pallas kernels  182 us (99%)
    pallas_call x1, Pallas kernels, local(): pl.pallas_call(finish, out_shape=(jax.ShapeDtypeStruct((K, D), f32), jax....  97.8 us
    pallas_call x1, Pallas kernels, local(): pl.pallas_call(kernel, out_shape=(jax.ShapeDtypeStruct((K, D), f32), jax....  84.7 us

profile of v2, /device:TPU:1, one launch (start us, length us, event | category | flops | bytes accessed | tf_op | source)
XLA Modules:
  0.0 183.2 jit_solution(16254312707190323452)
XLA Ops:
  0.6 84.7 %shard_map.41 = (f32[1024,768]{1,0:T(8,128)}, f32[16,256]{1,0:T(8,128)}) custom-call(bf16[2048,768]{1,0:T(8,128)(2,1)} %e_hbm.1, f32[1024,768]{1,0:T(8,128)} %c_hbm.1), custom_call_target="tpu_custom_call" | custom-call | tf_op jit(solution)/shard_map/pallas_call | solution.py:450
  85.3 97.8 %shard_map.42 = (f32[1024,768]{1,0:T(8,128)}, f32[16,128]{1,0:T(8,128)}) custom-call(f32[1024,768]{1,0:T(8,128)} %get-tuple-element.6.c, f32[16,256]{1,0:T(8,128)} %get-tuple-element.7.tot), custom_call_target="tpu_custom_call" | custom-call | tf_op jit(solution)/shard_map/pallas_call | solution.py:485

commit v3 on v2

--- a/solution.py
+++ b/solution.py
@@ -114,11 +114,7 @@
     spread(0)
     tell(0)
 
-    @pl.loop(1, 7)
-    def _(t):
-        spread(t)
-
-    spread_whole()
+    spread(1)
 
     def got(u, half, q):
         remote(
@@ -344,26 +340,35 @@
     def _(k):
         prepare(rows(k * CHUNK, CHUNK))
 
+    told(0)
+    tell(1)
+
     def meanwhile(k):
         @pl.when(k == 0)
         def _():
-            told(0)
-            tell(1)
-
-        @pl.when(k == 1)
-        def _():
             told(1)
             tell(2)
 
+        @pl.when(k == 1)
+        def _():
+            told(2)
+            for h in range(2):
+                stats_first(0, h)
+
         forward(k)
+        spread(k + 2)
 
     pipelined(2, meanwhile)
     forward(2)
-    told(2)
+
+    @pl.loop(4, 6)
+    def _(t):
+        spread(t)
+
     for h in range(2):
-        stats_first(0, h)
-    for t in (3, 4):
-        forward(t)
+        stats_second(0, h)
+    forward(3)
+    spread(6)
 
     @pl.loop(4, 8)
     def _(g):
@@ -373,8 +378,8 @@
 
         @pl.when(g == 4)
         def _():
-            for h in range(2):
-                stats_second(0, h)
+            forward(4)
+            spread_whole()
 
             @pl.loop(5, 7)
             def _(t):
@@ -428,20 +433,23 @@
     out_t[...] = tot[1, 0:16, :]
 
 
-def finish(c, tot, out_c, out_l, sems):
-    copies = []
-    for k in range(8):
-        at = pl.ds(k * 128, 128)
-        copies.append(pltpu.make_async_copy(c.at[at], out_c.at[at], sems.at[k]))
-        copies[k].start()
+def finish(c, tot, out_c, out_l, hold, reads, writes):
+    blocks = [pl.ds(k * CHUNK, CHUNK) for k in range(K // CHUNK)]
+    ins = [pltpu.make_async_copy(c.at[at], hold.at[at], reads.at[k]) for k, at in enumerate(blocks)]
+    outs = [pltpu.make_async_copy(hold.at[at], out_c.at[at], writes.at[k]) for k, at in enumerate(blocks)]
+    for copy in ins:
+        copy.start()
     for h in range(2):
         value = (tot[h * 8 : h * 8 + 4, :] + jnp.log2(tot[h * 8 + 4 : h * 8 + 8, :])) * LN2
         for j in range(4):
             at = 8 * h + 2 * j
             out_l[at : at + 1, :] = value[j : j + 1, :128]
             out_l[at + 1 : at + 2, :] = value[j : j + 1, 128:]
-    for copy in copies:
-        copy.wait()
+    for read, write in zip(ins, outs):
+        read.wait()
+        write.start()
+    for write in outs:
+        write.wait()
 
 
 def local(embeddings, centroids):
@@ -487,7 +495,7 @@
         out_shape=(jax.ShapeDtypeStruct((K, D), f32), jax.ShapeDtypeStruct((16, 128), f32)),
         in_specs=[pl.BlockSpec(memory_space=pl.ANY), pl.BlockSpec(memory_space=vmem)],
         out_specs=(pl.BlockSpec(memory_space=pl.ANY), pl.BlockSpec(memory_space=vmem)),
-        scratch_shapes=[dma((8,))],
+        scratch_shapes=[vmem((K, D), f32), dma((8,)), dma((8,))],
         compiler_params=pltpu.CompilerParams(vmem_limit_bytes=60 << 20),
     )(new, stats)
     return new, logs.reshape(R)

time: 183 us -> 84.1 us (0.46)
  Pallas kernels: 182 us -> 83.1 us
    pallas_call x1, Pallas kernels: 97.8 us -> 4.1 us  [local(): pl.pallas_call(finish, out_shape=(jax.ShapeDtypeStruct((K, D), f32), jax....]
    pallas_call x1, Pallas kernels: 84.7 us -> 79 us  [local(): pl.pallas_call(kernel, out_shape=(jax.ShapeDtypeStruct((K, D), f32), jax....]
where the time goes in v3:
time: 84.1 us; the launch traced here: 83.9 us
  Pallas kernels  83.1 us (99%)
    pallas_call x1, Pallas kernels, local(): pl.pallas_call(kernel, out_shape=(jax.ShapeDtypeStruct((K, D), f32), jax....  79 us
    pallas_call x1, Pallas kernels, local(): pl.pallas_call(finish, out_shape=(jax.ShapeDtypeStruct((K, D), f32), jax....  4.1 us

profile of v3, /device:TPU:1, one launch (start us, length us, event | category | flops | bytes accessed | tf_op | source)
XLA Modules:
  0.0 83.9 jit_solution(9351339571411572841)
XLA Ops:
  0.6 79.0 %shard_map.41 = (f32[1024,768]{1,0:T(8,128)}, f32[16,256]{1,0:T(8,128)}) custom-call(bf16[2048,768]{1,0:T(8,128)(2,1)} %e_hbm.1, f32[1024,768]{1,0:T(8,128)} %c_hbm.1), custom_call_target="tpu_custom_call" | custom-call | tf_op jit(solution)/shard_map/pallas_call | solution.py:458
  79.6 4.1 %shard_map.42 = (f32[1024,768]{1,0:T(8,128)}, f32[16,128]{1,0:T(8,128)}) custom-call(f32[1024,768]{1,0:T(8,128)} %get-tuple-element.6.c, f32[16,256]{1,0:T(8,128)} %get-tuple-element.7.tot), custom_call_target="tpu_custom_call" | custom-call | tf_op jit(solution)/shard_map/pallas_call | solution.py:493

commit v4 on v3

--- a/solution.py
+++ b/solution.py
@@ -28,9 +28,9 @@
 
 
 def kernel(
-    e_hbm, c_hbm, out_c, out_t,
-    e, land, sb, c, cb, nrm, p, ml, z1, z2, tot, s, mass, rs, rsm, wbuf, d0, d1,
-    esem, csem, osem, gsend, grecv, s1s, s1r, s2s, s2r, fs, fr, rss, rsr, ms, mr, ags, agr, relay,
+    e_hbm, c_hbm, c, out_l,
+    e, land, sb, cb, nrm, p, ml, z1, z2, tot, s, mass, rs, rsm, wbuf, d0, d1,
+    esem, csem, gsend, grecv, s1s, s1r, s2s, s2r, fs, fr, rss, rsr, ms, mr, ags, agr, relay,
 ):
     dp, ct = lax.axis_index("dp"), lax.axis_index("cent")
     core, xlo = lax.rem(dp, 2), dp // 2
@@ -233,7 +233,7 @@
         d0[...] = dot(g)
         soft(d0, g)
 
-    def weigh(it, u0, n, at):
+    def weigh(it, u0, n, at, slot):
         total = jnp.zeros((BLOCK, 128), jnp.float32)
         for j in range(n):
             row = stat_row(u0 + j)
@@ -241,19 +241,20 @@
             w = (p[u0 + j, at, :] * part).astype(jnp.bfloat16)
             wide = w.astype(jnp.float32)
             total += wide[:, :128] + wide[:, 128:]
-            wbuf[:, j * UNIT : (j + 1) * UNIT] = w
+            wbuf[slot, :, j * UNIT : (j + 1) * UNIT] = w
         block = e[rows(u0 * UNIT, n * UNIT), :]
-        return jnp.dot(wbuf[:, : n * UNIT], block, preferred_element_type=jnp.float32), total
-
-    def weigh_half(it, side, h, at):
-        add, total = weigh(it, 8 * side + 4 * h, 4, at)
+        return jnp.dot(wbuf[slot], block, preferred_element_type=jnp.float32), total
+
+    def weigh_half(it, side, h, at, slot):
+        add, total = weigh(it, 8 * side + 4 * h, 4, at, slot)
         s[side, at, :] = add if h == 0 else s[side, at, :] + add
         mass[side, at, :] = total if h == 0 else mass[side, at, :] + total
 
     def weigh_own(it, h):
-        @pl.loop(0, K // BLOCK)
+        @pl.loop(0, K // BLOCK // 2)
         def _(k):
-            weigh_half(it, 0, h, rows(k * BLOCK, BLOCK))
+            for j in range(2):
+                weigh_half(it, 0, h, rows((2 * k + j) * BLOCK, BLOCK), j)
 
     mine, theirs = core * H, (1 - core) * H
     n = H // BLOCK
@@ -261,7 +262,7 @@
     def update(it):
         def finish_sums(at):
             for h in range(2):
-                weigh_half(it, 1, h, at)
+                weigh_half(it, 1, h, at, h)
             return s[0, at, :] + s[1, at, :], mass[0, at, :] + mass[1, at, :]
 
         def give(k):
@@ -274,8 +275,7 @@
 
         def spread_new(start, i):
             at = rows(start + i * CHUNK, CHUNK)
-            dst = c if it == 0 else out_c
-            return remote(c.at[at], dst.at[at], ags.at[it * 4 + i], agr.at[it * 4 + i], twin)
+            return remote(c.at[at], c.at[at], ags.at[it * 4 + i], agr.at[it * 4 + i], twin)
 
         @pl.loop(0, n)
         def _(k):
@@ -302,8 +302,6 @@
                 spread_new(mine, 2 * k + j).start()
                 if it == 0:
                     prepare(sub)
-            if it == 1:
-                pltpu.make_async_copy(c.at[at], out_c.at[at], osem.at[k]).start()
 
         @pl.loop(0, n)
         def _(k):
@@ -313,9 +311,6 @@
                 spread_new(theirs, 2 * k + j).wait()
                 if it == 0:
                     prepare(rows(theirs + k * BLOCK + j * CHUNK, CHUNK))
-            if it == 1:
-                at = rows(mine + k * BLOCK, BLOCK)
-                pltpu.make_async_copy(c.at[at], out_c.at[at], osem.at[k]).wait()
 
     def pipelined(pairs, hook):
         d0[...] = dot(0)
@@ -340,6 +335,10 @@
     def _(k):
         prepare(rows(k * CHUNK, CHUNK))
 
+    @pl.loop(2, 7)
+    def _(t):
+        spread(t)
+
     told(0)
     tell(1)
 
@@ -356,19 +355,14 @@
                 stats_first(0, h)
 
         forward(k)
-        spread(k + 2)
 
     pipelined(2, meanwhile)
-    forward(2)
-
-    @pl.loop(4, 6)
-    def _(t):
-        spread(t)
-
+    for t in (2, 3):
+        forward(t)
     for h in range(2):
         stats_second(0, h)
-    forward(3)
-    spread(6)
+    spread_whole()
+    forward(4)
 
     @pl.loop(4, 8)
     def _(g):
@@ -378,13 +372,12 @@
 
         @pl.when(g == 4)
         def _():
-            forward(4)
-            spread_whole()
-
             @pl.loop(5, 7)
             def _(t):
                 forward(t)
 
+        @pl.when(g == 5)
+        def _():
             for h in range(2):
                 stats_last(0, h)
                 weigh_own(0, h)
@@ -430,41 +423,26 @@
                 remote(ref, ref, s2s.at[(it * 2 + h) * 8 + k], s2r.at[0], twin).wait_send()
             share(it, h).wait_send()
 
-    out_t[...] = tot[1, 0:16, :]
-
-
-def finish(c, tot, out_c, out_l, hold, reads, writes):
-    blocks = [pl.ds(k * CHUNK, CHUNK) for k in range(K // CHUNK)]
-    ins = [pltpu.make_async_copy(c.at[at], hold.at[at], reads.at[k]) for k, at in enumerate(blocks)]
-    outs = [pltpu.make_async_copy(hold.at[at], out_c.at[at], writes.at[k]) for k, at in enumerate(blocks)]
-    for copy in ins:
-        copy.start()
     for h in range(2):
-        value = (tot[h * 8 : h * 8 + 4, :] + jnp.log2(tot[h * 8 + 4 : h * 8 + 8, :])) * LN2
+        value = (tot[1, h * 8 : h * 8 + 4, :] + jnp.log2(tot[1, h * 8 + 4 : h * 8 + 8, :])) * LN2
         for j in range(4):
             at = 8 * h + 2 * j
             out_l[at : at + 1, :] = value[j : j + 1, :128]
             out_l[at + 1 : at + 2, :] = value[j : j + 1, 128:]
-    for read, write in zip(ins, outs):
-        read.wait()
-        write.start()
-    for write in outs:
-        write.wait()
 
 
 def local(embeddings, centroids):
     f32, bf16, dma = jnp.float32, jnp.bfloat16, pltpu.SemaphoreType.DMA
     vmem = pltpu.VMEM
-    new, stats = pl.pallas_call(
+    new, logs = pl.pallas_call(
         kernel,
-        out_shape=(jax.ShapeDtypeStruct((K, D), f32), jax.ShapeDtypeStruct((16, UNIT), f32)),
+        out_shape=(vmem((K, D), f32), vmem((16, 128), f32)),
         in_specs=[pl.BlockSpec(memory_space=pl.ANY)] * 2,
-        out_specs=(pl.BlockSpec(memory_space=pl.ANY), pl.BlockSpec(memory_space=pltpu.VMEM)),
+        out_specs=(pl.BlockSpec(memory_space=vmem), pl.BlockSpec(memory_space=vmem)),
         scratch_shapes=[
             vmem((2 * R, D), bf16),
             vmem((R, D), f32),
             vmem((768, D), f32),
-            vmem((K, D), f32),
             vmem((K, D), bf16),
             vmem((K, 128), f32),
             vmem((16, K, UNIT), f32),
@@ -476,10 +454,10 @@
             vmem((2, K, 128), f32),
             vmem((H, D), f32),
             vmem((H, 128), f32),
-            vmem((BLOCK, 4 * UNIT), bf16),
+            vmem((2, BLOCK, 4 * UNIT), bf16),
             vmem((K, 2 * UNIT), f32),
             vmem((K, 2 * UNIT), f32),
-            dma, dma, dma((4,)),
+            dma, dma,
             dma((64,)), dma((64,)),
             dma((32,)), dma((32,)), dma((32,)), dma((32,)),
             dma((4,)), dma((4,)),
@@ -490,14 +468,6 @@
             collective_id=0, has_side_effects=True, vmem_limit_bytes=54 << 20
         ),
     )(embeddings, centroids)
-    new, logs = pl.pallas_call(
-        finish,
-        out_shape=(jax.ShapeDtypeStruct((K, D), f32), jax.ShapeDtypeStruct((16, 128), f32)),
-        in_specs=[pl.BlockSpec(memory_space=pl.ANY), pl.BlockSpec(memory_space=vmem)],
-        out_specs=(pl.BlockSpec(memory_space=pl.ANY), pl.BlockSpec(memory_space=vmem)),
-        scratch_shapes=[vmem((K, D), f32), dma((8,)), dma((8,))],
-        compiler_params=pltpu.CompilerParams(vmem_limit_bytes=60 << 20),
-    )(new, stats)
     return new, logs.reshape(R)
 
 

time: 84.1 us -> 80.7 us (0.960)
  Pallas kernels: 83.1 us -> 77.7 us
  local copies, waits for them, and re-layouts: 0 us -> 2.27 us
    pallas_call x2 -> x1, Pallas kernels: 83.1 us -> 77.7 us  [local(): pl.pallas_call(kernel, out_shape=(vmem((K, D), f32), vmem((16, 128), f32)...]
    unnamed x0 -> x2, local copies, waits for them, and re-layouts: none -> 2.27 us
where the time goes in v4:
time: 80.7 us; the launch traced here: 80.6 us
  Pallas kernels  77.7 us (96%)
  local copies, waits for them, and re-layouts  2.27 us (3%)
    pallas_call x1, Pallas kernels, local(): pl.pallas_call(kernel, out_shape=(vmem((K, D), f32), vmem((16, 128), f32)...  77.7 us
    unnamed x2, local copies, waits for them, and re-layouts  2.27 us

profile of v4, /device:TPU:1, one launch (start us, length us, event | category | flops | bytes accessed | tf_op | source)
XLA Modules:
  0.0 80.6 jit_solution(14413463337041803350)
XLA Ops:
  0.6 77.7 %shard_map.41 = (f32[1024,768]{1,0:T(8,128)S(1)}, f32[16,128]{1,0:T(8,128)S(1)}) custom-call(bf16[2048,768]{1,0:T(8,128)(2,1)} %e_hbm.1, f32[1024,768]{1,0:T(8,128)} %c_hbm.1), custom_call_target="tpu_custom_call" | custom-call | tf_op jit(solution)/shard_map/pallas_call | solution.py:437
  78.4 1.7 %copy.6 = f32[1024,768]{1,0:T(8,128)} copy(f32[1024,768]{1,0:T(8,128)S(1)} %get-tuple-element.6) | data formatting | bytes 6291456
  80.0 0.6 copy.7

commit v5 on v4

--- a/solution.py
+++ b/solution.py
@@ -213,6 +213,10 @@
 
     def dot(g):
         return lax.dot_general(cb[...], e[rows(g * 512, 512), :], NT, preferred_element_type=jnp.float32)
+
+    def dot_first(start):
+        at = rows(start, H)
+        d0[at, :] = lax.dot_general(cb[at, :], e[pl.ds(0, 512), :], NT, preferred_element_type=jnp.float32)
 
     def stat_row(u):
         return (u // 4) * 8 + lax.rem(u, 4)
@@ -303,6 +307,9 @@
                 if it == 0:
                     prepare(sub)
 
+        if it == 0:
+            dot_first(mine)
+
         @pl.loop(0, n)
         def _(k):
             for copy in give(k):
@@ -312,13 +319,18 @@
                 if it == 0:
                     prepare(rows(theirs + k * BLOCK + j * CHUNK, CHUNK))
 
-    def pipelined(pairs, hook):
-        d0[...] = dot(0)
+        if it == 0:
+            dot_first(theirs)
+
+    def pipelined(pairs, mid, hook, ready):
+        if not ready:
+            d0[...] = dot(0)
 
         @pl.loop(0, pairs)
         def _(k):
             d1[...] = dot(2 * k + 1)
             soft(d0, 2 * k)
+            mid(k)
 
             @pl.when(k < pairs - 1)
             def _():
@@ -343,6 +355,8 @@
     tell(1)
 
     def meanwhile(k):
+        forward(k)
+
         @pl.when(k == 0)
         def _():
             told(1)
@@ -351,12 +365,10 @@
         @pl.when(k == 1)
         def _():
             told(2)
-            for h in range(2):
-                stats_first(0, h)
-
-        forward(k)
-
-    pipelined(2, meanwhile)
+
+    pipelined(2, meanwhile, lambda k: None, False)
+    for h in range(2):
+        stats_first(0, h)
     for t in (2, 3):
         forward(t)
     for h in range(2):
@@ -397,7 +409,7 @@
         def _():
             stats_second(1, 0)
 
-    pipelined(4, between)
+    pipelined(4, lambda k: None, between, True)
     stats_second(1, 1)
     for h in range(2):
         stats_last(1, h)

time: 80.7 us -> 79.8 us (0.989)
  Pallas kernels: 77.7 us -> 76.8 us
    pallas_call x1, Pallas kernels: 77.7 us -> 76.8 us  [local(): pl.pallas_call(kernel, out_shape=(vmem((K, D), f32), vmem((16, 128), f32)...]
where the time goes in v5:
time: 79.8 us; the launch traced here: 79.7 us
  Pallas kernels  76.8 us (96%)
  local copies, waits for them, and re-layouts  2.27 us (3%)
    pallas_call x1, Pallas kernels, local(): pl.pallas_call(kernel, out_shape=(vmem((K, D), f32), vmem((16, 128), f32)...  76.8 us
    unnamed x2, local copies, waits for them, and re-layouts  2.27 us

profile of v5, /device:TPU:1, one launch (start us, length us, event | category | flops | bytes accessed | tf_op | source)
XLA Modules:
  0.0 79.7 jit_solution(10749827971646526079)
XLA Ops:
  0.6 76.8 %shard_map.41 = (f32[1024,768]{1,0:T(8,128)S(1)}, f32[16,128]{1,0:T(8,128)S(1)}) custom-call(bf16[2048,768]{1,0:T(8,128)(2,1)} %e_hbm.1, f32[1024,768]{1,0:T(8,128)} %c_hbm.1), custom_call_target="tpu_custom_call" | custom-call | tf_op jit(solution)/shard_map/pallas_call | solution.py:449
  77.4 1.7 %copy.6 = f32[1024,768]{1,0:T(8,128)} copy(f32[1024,768]{1,0:T(8,128)S(1)} %get-tuple-element.6) | data formatting | bytes 6291456
  79.1 0.6 copy.7

commit v6 on v5

--- a/solution.py
+++ b/solution.py
@@ -214,8 +214,8 @@
     def dot(g):
         return lax.dot_general(cb[...], e[rows(g * 512, 512), :], NT, preferred_element_type=jnp.float32)
 
-    def dot_first(start):
-        at = rows(start, H)
+    def dot_first(start, size):
+        at = rows(start, size)
         d0[at, :] = lax.dot_general(cb[at, :], e[pl.ds(0, 512), :], NT, preferred_element_type=jnp.float32)
 
     def stat_row(u):
@@ -308,7 +308,7 @@
                     prepare(sub)
 
         if it == 0:
-            dot_first(mine)
+            dot_first(mine, H)
 
         @pl.loop(0, n)
         def _(k):
@@ -318,9 +318,8 @@
                 spread_new(theirs, 2 * k + j).wait()
                 if it == 0:
                     prepare(rows(theirs + k * BLOCK + j * CHUNK, CHUNK))
-
-        if it == 0:
-            dot_first(theirs)
+                    if j == 1:
+                        dot_first(theirs + k * BLOCK, BLOCK)
 
     def pipelined(pairs, mid, hook, ready):
         if not ready:

time: 79.8 us -> 79.5 us (level)
  no operation moved by 1% of the time
where the time goes in v6:
time: 79.5 us; the launch traced here: 79.4 us
  Pallas kernels  76.5 us (96%)
  local copies, waits for them, and re-layouts  2.27 us (3%)
    pallas_call x1, Pallas kernels, local(): pl.pallas_call(kernel, out_shape=(vmem((K, D), f32), vmem((16, 128), f32)...  76.5 us
    unnamed x2, local copies, waits for them, and re-layouts  2.27 us

profile of v6, /device:TPU:1, one launch (start us, length us, event | category | flops | bytes accessed | tf_op | source)
XLA Modules:
  0.0 79.4 jit_solution(8718386468677569640)
XLA Ops:
  0.6 76.5 %shard_map.41 = (f32[1024,768]{1,0:T(8,128)S(1)}, f32[16,128]{1,0:T(8,128)S(1)}) custom-call(bf16[2048,768]{1,0:T(8,128)(2,1)} %e_hbm.1, f32[1024,768]{1,0:T(8,128)} %c_hbm.1), custom_call_target="tpu_custom_call" | custom-call | tf_op jit(solution)/shard_map/pallas_call | solution.py:448
  77.2 1.7 %copy.6 = f32[1024,768]{1,0:T(8,128)} copy(f32[1024,768]{1,0:T(8,128)S(1)} %get-tuple-element.6) | data formatting | bytes 6291456
  78.8 0.6 copy.7
